TPU v7x, 512 devices: a whole 4x8x8 slice. The times are simulated.
512 devices in a mesh: trow: 8 (over y), tcol: 8 (over x, z_lo), dp: 8 (over z_hi, core).
Axes of the slice: x: 4, y: 8, z: 8 (z_hi: 4, z_lo: 2; z = z_hi * 2 + z_lo), core: 2. Of those that a mesh axis runs over, the one named last changes fastest.
Arguments:
- embeds: bfloat16 [8192, 1024], P('dp'), may hold values from -6 to 6
- frequencies: bfloat16 [1024, 8192], P(None, ('trow', 'tcol')), may hold values from -0.5 to 0.5
- phases: float32 [8192], P(('trow', 'tcol')), may hold values from -3.140625 to 3.140625
- labels: int32 [8192], P('dp'), may hold values from 0 to 999
- weights: float32 [8192, 1000], P(('tcol', 'dp'), 'trow'), may hold values from -6 to 6
Outputs:
- gram_matrix: float32 [8192, 8192], P(('trow', 'dp'), 'tcol')
- new_weights: float32 [8192, 1000], P(('tcol', 'dp'), 'trow')
All inputs are finite; a program needn't handle non-finite values.
Results may differ from a plain program's by a relative error of at most 0.023.
Values may be sent and summed in bfloat16 or wider, within the bound.
A program may use at most 64 MiB of HBM per device.

v0:
```python
import jax
import jax.numpy as jnp
from jax import lax
from jax.sharding import PartitionSpec as P

C = 1000


ROOT_TWO = 1.4142135623730951
RIDGE = 0.5
STEP_RATE = 0.5


def copy_for_each(array, axis):
    size = lax.axis_size(axis)
    return lax.all_to_all(
        jnp.broadcast_to(array[None], (size, *array.shape)), axis, 0, 0, tiled=True
    )


def laid_out(parts, dim):
    dims = list(parts.shape[1:])
    dims[dim] *= parts.shape[0]
    return jnp.moveaxis(parts, 0, dim).reshape(dims)


def gather_directly(array, axis, dim):
    parts = copy_for_each(array, axis)
    return laid_out(parts, dim)


def padded_to(lines, size):
    spare = -lines.shape[0] % size
    if not spare:
        return lines
    return jnp.concatenate([lines, jnp.zeros((spare, *lines.shape[1:]), lines.dtype)])


def broadcast_by_parts(array, axis, root):
    lines = jnp.where(lax.axis_index(axis) == root, array, jnp.zeros_like(array)).reshape(
        -1, *array.shape[1:][-1:]
    )
    padded = padded_to(lines, lax.axis_size(axis))
    own = lax.psum_scatter(padded, axis, scatter_dimension=0, tiled=True)
    return lax.all_gather(own, axis, axis=0, tiled=True)[: len(lines)].reshape(array.shape)


def split_up(array, dim, size):
    dims = array.shape
    parts = array.reshape(*dims[:dim], size, dims[dim] // size, *dims[dim + 1 :])
    return jnp.moveaxis(parts, dim, 0)


def sum_at_owner(array, axis, dim):
    parts = split_up(array, dim, lax.axis_size(axis))
    arrived = lax.all_to_all(parts, axis, split_axis=0, concat_axis=0, tiled=True)
    return arrived.astype(jnp.float32).sum(axis=0)


def of_everyone(array, axis):
    everything = copy_for_each(array, axis)
    return jnp.sum(everything.astype(jnp.float32), axis=0)


def broadcast(array, axis, root):
    return lax.dynamic_index_in_dim(lax.all_gather(array, axis), root, 0, keepdims=False)


def featurize(embeds, frequencies, phases):
    angles = jnp.dot(embeds, frequencies, preferred_element_type=jnp.float32) + phases
    return (ROOT_TWO * jnp.cos(angles)).astype(jnp.bfloat16)


def shards(embeds, frequencies, phases, labels, weights):
    rows_here = embeds.shape[0]
    n_row = lax.axis_size("trow")
    n_dp = lax.axis_size("dp")
    row_idx = lax.axis_index("trow")
    col_idx = lax.axis_index("tcol")
    dp_idx = lax.axis_index("dp")
    total_rows = rows_here * n_dp
    contract = (((0,), (0,)), ((), ()))
    own_part = featurize(embeds, frequencies, phases)
    left_feats = gather_directly(own_part, "tcol", 1)
    right_feats = broadcast_by_parts(left_feats, "trow", col_idx)
    tile_width = left_feats.shape[1]
    sub_rows = tile_width // n_dp
    gram_part = lax.psum_scatter(
        (
            lax.dot_general(left_feats, right_feats, contract, preferred_element_type=jnp.float32)
            / total_rows
        ).astype(jnp.bfloat16),
        "dp",
        scatter_dimension=0,
        tiled=True,
    ).astype(jnp.float32)
    global_rows = row_idx * tile_width + dp_idx * sub_rows + jnp.arange(sub_rows, dtype=jnp.int32)
    global_cols = col_idx * tile_width + jnp.arange(tile_width, dtype=jnp.int32)
    gram_rows = gram_part + RIDGE * (global_rows[:, None] == global_cols[None, :]).astype(
        jnp.float32
    )
    class_width = weights.shape[1]
    class_ids = row_idx * class_width + jnp.arange(class_width, dtype=jnp.int32)
    onehot = (labels[:, None] == class_ids[None, :]).astype(jnp.bfloat16)
    label_term = lax.dot_general(
        right_feats, onehot, contract, preferred_element_type=jnp.float32
    ) * (C / total_rows)
    label_rows = sum_at_owner(label_term.astype(jnp.bfloat16), "dp", 0)
    gram_three = gram_rows.astype(jnp.bfloat16).reshape(sub_rows, n_dp, sub_rows)
    block_ids = jnp.arange(n_row, dtype=jnp.int32)
    local_weights = weights.astype(jnp.bfloat16)[None]
    pieces = lax.all_gather(local_weights, ("trow", "dp"), axis=0, tiled=True)
    positions = jnp.arange(pieces.shape[0], dtype=jnp.int32)
    sub_index = positions % n_dp
    owner_index = positions // n_dp
    chosen = jnp.take(gram_three, sub_index, axis=1)
    products = jnp.einsum("rpk,pkc->rpc", chosen, pieces, preferred_element_type=jnp.float32)
    placing = (owner_index[:, None] == block_ids[None, :]).astype(jnp.float32)
    folded = jnp.einsum("rpc,pi->ric", products, placing)
    curv_local = folded.reshape(sub_rows, n_row * class_width)
    diag_block = lax.dynamic_slice_in_dim(gram_rows, dp_idx * sub_rows, sub_rows, 1)
    diag_local = jnp.diagonal(diag_block) * (row_idx == col_idx).astype(jnp.float32)
    row_total = of_everyone(curv_local.astype(jnp.bfloat16), "tcol").astype(jnp.float32)
    received, diag_vals = (
        broadcast(row_total.astype(jnp.bfloat16), "trow", col_idx).astype(row_total.dtype),
        broadcast(diag_local.astype(jnp.bfloat16), "trow", col_idx).astype(diag_local.dtype),
    )
    curv_mine = lax.dynamic_slice_in_dim(received, row_idx * class_width, class_width, 1)
    updated = weights - STEP_RATE * (curv_mine - label_rows) / diag_vals[:, None]
    return (gram_rows, updated)


def solution(mesh):
    return jax.shard_map(
        shards,
        mesh=mesh,
        in_specs=(
            P("dp", None),
            P(None, ("trow", "tcol")),
            P(("trow", "tcol")),
            P("dp"),
            P(("tcol", "dp"), "trow"),
        ),
        out_specs=(P(("trow", "dp"), "tcol"), P(("tcol", "dp"), "trow")),
        check_vma=False,
    )
```

profile of v0, /device:TPU:1, one launch (start us, length us, event | category | flops | bytes accessed | tf_op | source)
XLA Modules:
  0.0 344.3 jit_solution(17416006484841058802)
XLA Ops:
  8.0 0.0 copy-start
  8.0 1.6 copy-done
  9.6 3.3 fusion.5
  12.9 0.1 copy.15
  13.1 1.6 broadcast_in_dim.20
  14.7 6.7 %all-to-all-start = ((bf16[8,1024,128]{1,2,0:T(8,128)(2,1)}), bf16[8,1024,128]{1,2,0:T(8,128)(2,1)}, u32[]{:S(2)}, u32[]{:S(2)}) async-start(bf16[8,1024,128]{1,2,0:T(8,128)(2,1)} %broadcast_in_dim.20), calls=%async_computation | async-start | bytes 4194304 | tf_op jit(solution)/shard_map/all_to_all | solution.py:16
  21.4 0.0 reduce-scatter.7.cloned.1.call-start
  21.4 22.6 %all-to-all-done = bf16[8,1024,128]{1,2,0:T(8,128)(2,1)} async-done(((bf16[8,1024,128]{1,2,0:T(8,128)(2,1)}), bf16[8,1024,128]{1,2,0:T(8,128)(2,1)}, u32[]{:S(2)}, u32[]{:S(2)}) %all-to-all-start) | async-done | bytes 2097184 | tf_op jit(solution)/shard_map/all_to_all | solution.py:16
  44.0 3.0 broadcast_select_fusion
  47.1 3.9 %copy.20 = bf16[1024,1024]{1,0:T(8,128)(2,1)} copy(bf16[1024,1024]{0,1:T(8,128)(2,1)} %broadcast_select_fusion) | data formatting | bytes 4194304
  51.0 0.0 reduce-scatter.7.cloned.1.call-update
  51.1 0.0 all-gather.8.cloned.1.call-start
  51.1 47.2 %reduce-scatter.7.cloned.1.call-done = bf16[128,1024]{1,0:T(8,128)(2,1)} async-done(((bf16[1024,1024]{1,0:T(8,128)(2,1)}), bf16[128,1024]{1,0:T(8,128)(2,1)}) %reduce-scatter.7.cloned.1.call-update) | async-done | bytes 262160
  98.4 1.8 copy.21
  100.2 0.0 all-gather.8.cloned.1.call-update
  100.2 0.0 reduce-scatter.5.cloned.1.call-start
  100.2 50.1 %all-gather.8.cloned.1.call-done = bf16[1024,1024]{0,1:T(8,128)(2,1)} async-done(((bf16[128,1024]{0,1:T(8,128)(2,1)}), bf16[1024,1024]{0,1:T(8,128)(2,1)}) %all-gather.8.cloned.1.call-update) | async-done | bytes 2097168 | tf_op jit(solution)/shard_map/all_gather | solution.py:45
  150.3 5.9 %multiply_convert_fusion = bf16[1024,1024]{1,0:T(8,128)(2,1)} fusion(bf16[1024,1024]{0,1:T(8,128)(2,1)} %bitcast.1, bf16[1024,1024]{0,1:T(8,128)(2,1)} %all-gather.8.cloned.1.call-done), kind=kOutput, calls=%fused_computation.2 | convolution fusion | flops 2149580800 | bytes 6291456 | tf_op jit(solution)/shard_map/dot_general | solution.py:90
  156.2 0.0 reduce-scatter.5.cloned.1.call-update
  156.2 0.0 all-gather.10.cloned.1.call-start
  156.3 0.8 copy-done.2
  157.1 0.6 convert_element_type.73
  157.7 0.0 all-gather.10.cloned.1.call-update
  157.7 0.0 all-gather.12.cloned.1.call-start
  157.8 46.7 %reduce-scatter.5.cloned.1.call-done = bf16[128,1024]{1,0:T(8,128)(2,1)} async-done(((bf16[1024,1024]{1,0:T(8,128)(2,1)}), bf16[128,1024]{1,0:T(8,128)(2,1)}) %reduce-scatter.5.cloned.1.call-update) | async-done | bytes 262160 | tf_op jit(solution)/shard_map/reduce_scatter | solution.py:88
  204.6 1.1 convert_bitcast_fusion
  205.7 0.0 copy-start.1
  205.7 2.1 gather_fusion
  207.9 41.6 %all-gather.10.cloned.1.call-done = bf16[8192,125]{1,0:T(8,128)(2,1)} async-done(((bf16[128,125]{1,0:T(8,128)(2,1)}), bf16[8192,125]{1,0:T(8,128)(2,1)}) %all-gather.10.cloned.1.call-update) | async-done | bytes 2048016 | tf_op jit(solution)/shard_map/all_gather | solution.py:112
  249.5 4.3 %convolution_bitcast_fusion = bf16[128,64,125]{2,0,1:T(8,128)(2,1)} fusion(bf16[64,128,125]{2,1,0:T(8,128)(2,1)} %bitcast.56, bf16[64,128,128]{2,1,0:T(8,128)(2,1)} %gather_fusion, pred[64]{0:T(512)(128)(4,1)S(1)} %compare_and_fusion), kind=kOutput, calls=%fused_computation.3 | convolution fusion | flops 263192576 | bytes 6193216 | tf_op jit(solution)/shard_map/rpk,pkc->rpc/dot_general | solution.py:117
  253.8 4.1 %copy.17 = bf16[128,64,125]{0,1,2:T(8,128)(2,1)} copy(bf16[128,64,125]{2,0,1:T(8,128)(2,1)} %convolution_bitcast_fusion) | data formatting | bytes 4096000 | tf_op jit(solution)/shard_map/rpk,pkc->rpc/transpose | solution.py:117
  257.9 1.9 fusion.7
  259.9 0.1 convert_element_type.76
  260.0 0.3 broadcast_in_dim.27
  260.3 29.7 %all_to_all.15 = bf16[8,128,1000]{1,2,0:T(8,128)(2,1)} all-to-all(bf16[8,128,1000]{1,2,0:T(8,128)(2,1)S(1)} %broadcast_in_dim.27), channel_id=1, replica_groups=mesh['trow'=8,'tcol'=8,'dp'=8] {'tcol'}, dimensions={0} | all-to-all | bytes 4096000 | tf_op jit(solution)/shard_map/all_to_all | solution.py:16
  290.0 2.6 reduce_sum.21
  292.6 0.0 all-gather.12.cloned.1.call-update
  292.7 3.1 fusion.6
  295.8 5.6 %all-to-all-start.2 = ((bf16[8,128,125]{2,1,0:T(8,128)(2,1)}), bf16[8,128,125]{2,1,0:T(8,128)(2,1)S(1)}, u32[]{:S(2)}, u32[]{:S(2)}) async-start(bf16[8,128,125]{2,1,0:T(8,128)(2,1)} %bitcast.10), calls=%async_computation.3 | async-start | bytes 524288 | tf_op jit(solution)/shard_map/all_to_all | solution.py:56
  301.4 10.3 %all-to-all-done.2 = bf16[8,128,125]{2,1,0:T(8,128)(2,1)S(1)} async-done(((bf16[8,128,125]{2,1,0:T(8,128)(2,1)}), bf16[8,128,125]{2,1,0:T(8,128)(2,1)S(1)}, u32[]{:S(2)}, u32[]{:S(2)}) %all-to-all-start.2) | async-done | bytes 256032 | tf_op jit(solution)/shard_map/all_to_all | solution.py:56
  311.7 0.1 convert_reduce_fusion
  311.8 1.2 gather_fusion.1
  313.0 12.0 %all-gather.3 = bf16[8,1,128]{2,1,0:T(2,128)(2,1)S(1)} all-gather(bf16[1,1,128]{2,1,0:T(2,128)(2,1)S(1)} %convert_bitcast_fusion.1), channel_id=4, replica_groups=mesh['trow'=8,'tcol'=8,'dp'=8] {'trow'}, dimensions={0}, use_global_device_ids=true | all-gather | bytes 2304 | tf_op jit(solution)/shard_map/all_gather | solution.py:66
  325.1 9.1 %all-gather.12.cloned.1.call-done = bf16[1024,1000]{0,1:T(8,128)(2,1)} async-done(((bf16[128,1000]{0,1:T(8,128)(2,1)}), bf16[1024,1000]{0,1:T(8,128)(2,1)}) %all-gather.12.cloned.1.call-update) | async-done | bytes 2048016 | tf_op jit(solution)/shard_map/all_gather | solution.py:66
  334.1 2.2 copy.23
  336.3 0.1 dynamic-slice_convert_fusion
  336.4 0.1 copy.19
  336.5 0.7 fusion.14
  (17 shorter events, 0.2 us)
Async XLA Ops:
  8.0 1.6 copy-start
  14.7 29.3 %all-to-all-start = ((bf16[8,1024,128]{1,2,0:T(8,128)(2,1)}), bf16[8,1024,128]{1,2,0:T(8,128)(2,1)}, u32[]{:S(2)}, u32[]{:S(2)}) async-start(bf16[8,1024,128]{1,2,0:T(8,128)(2,1)} %broadcast_in_dim.20), calls=%async_computation | async-start | bytes 4194304 | tf_op jit(solution)/shard_map/all_to_all | solution.py:16
  21.4 77.0 %reduce-scatter.7.cloned.1.call-start = ((), (), s32[]{:S(2)}) async-start(), calls=%async_computation.9 | async-start | bytes 2359296
  51.1 99.2 %all-gather.8.cloned.1.call-start = ((), (), s32[]{:S(2)}) async-start(), calls=%async_computation.5 | async-start | bytes 2359296 | tf_op jit(solution)/shard_map/all_gather | solution.py:45
  100.2 104.4 %reduce-scatter.5.cloned.1.call-start = ((), (), s32[]{:S(2)}) async-start(), calls=%async_computation.6 | async-start | bytes 2359296 | tf_op jit(solution)/shard_map/reduce_scatter | solution.py:88
  156.2 0.8 copy-start.2
  156.2 93.3 %all-gather.10.cloned.1.call-start = ((), (), s32[]{:S(2)}) async-start(), calls=%async_computation.7 | async-start | bytes 2129920 | tf_op jit(solution)/shard_map/all_gather | solution.py:112
  157.7 176.4 %all-gather.12.cloned.1.call-start = ((), (), s32[]{:S(2)}) async-start(), calls=%async_computation.8 | async-start | bytes 2304000 | tf_op jit(solution)/shard_map/all_gather | solution.py:66
  205.7 106.1 %copy-start.1 = (f32[128,1024]{1,0:T(8,128)}, f32[128,1024]{1,0:T(8,128)S(1)}, u32[]{:S(2)}) copy-start(f32[128,1024]{1,0:T(8,128)S(1)} %get-tuple-element.3) | copy-start | bytes 1572868
  290.0 2.7 copy-start.3
  295.8 15.9 %all-to-all-start.2 = ((bf16[8,128,125]{2,1,0:T(8,128)(2,1)}), bf16[8,128,125]{2,1,0:T(8,128)(2,1)S(1)}, u32[]{:S(2)}, u32[]{:S(2)}) async-start(bf16[8,128,125]{2,1,0:T(8,128)(2,1)} %bitcast.10), calls=%async_computation.3 | async-start | bytes 524288 | tf_op jit(solution)/shard_map/all_to_all | solution.py:56
Sparse Core Ops, SparseCore 0:
  51.2 47.1 reduce-scatter.6
  100.9 49.3 all-gather.7
  156.4 48.1 reduce-scatter.4
  292.8 41.2 all-gather.11
Sparse Core Ops, SparseCore 1:
  160.6 88.9 all-gather.9
where the time goes:
time: 349 us; the launch traced here: 344 us
  waiting for transfers between devices  228 us (65%)
  blocking collectives  41.7 us (12%)
  local copies, waits for them, and re-layouts  20.1 us (6%)
  matrix products  18.6 us (5%)
  between operations  15.4 us (4%)
  starting transfers between devices  12.4 us (4%)
  other arithmetic  8.31 us (2%)
    all_gather x1, waiting for transfers between devices, broadcast_by_parts(): lax.all_gather(own, axis, axis=0, tiled=True)[:len(lines)]  50.1 us
    unnamed x6, waiting for transfers between devices  47.3 us
    reduce_scatter x1, waiting for transfers between devices, shards(): lax.psum_scatter((lax.dot_general(left_feats, right_feats, contract, pref...  46.7 us
    all_gather x1, waiting for transfers between devices, shards(): pieces = lax.all_gather(local_weights, ('trow', 'dp'), axis=0, tiled=True)  41.6 us
    all_to_all x1, blocking collectives, copy_for_each(): lax.all_to_all(jnp.broadcast_to(array[None], (size, *array.shape)), axis,...  29.7 us
    all_to_all x1, waiting for transfers between devices, copy_for_each(): lax.all_to_all(jnp.broadcast_to(array[None], (size, *array.shape)), axis,...  22.6 us
    all_gather x1, blocking collectives, broadcast(): lax.all_gather(array, axis)  12 us
    all_to_all x1, waiting for transfers between devices, sum_at_owner(): lax.all_to_all(parts, axis, split_axis=0, concat_axis=0, tiled=True)  10.3 us
  transfers between devices with their start and end apart: 7, of which 7 were waited for; matrix products, arithmetic and copies ran while one was open for 2% of the time, Pallas kernels for 0%

commit v1 on v0

v1 whole, which is shorter than its diff:
```python
import jax
import jax.numpy as jnp
from jax import lax
from jax.experimental import pallas as pl
from jax.experimental.pallas import tpu as pltpu
from jax.sharding import PartitionSpec as P

C = 1000
RIDGE = 0.5
STEP_RATE = 0.5
MESH = pl.DeviceIdType.MESH
F32, BF16 = jnp.float32, jnp.bfloat16
NT = (((1,), (1,)), ((), ()))
NN = (((1,), (0,)), ((), ()))

N = 8
W = 128
ROWS = 1024
DIN = 1024
WIDE = DIN + 128
HALF = W // 2
CLS = 125
TOTAL = 8192
ND = 5
INV_PERIOD = 0.15915494309189535
COS = [
    1.4142135623730951 * q
    for q in (
        0.9999999890754399,
        -19.73920450099313,
        64.93911749956553,
        -85.45013994347214,
        60.16763282514798,
        -25.967602441408868,
        6.528658639370483,
    )
]


def dot(a, b, dims):
    return lax.dot_general(a, b, dims, preferred_element_type=F32)


def rem(a, b):
    return lax.rem(a, jnp.int32(b))


def place(a):
    return rem(a, 2) * 4 + lax.div(a, jnp.int32(2))


def rows(i, size):
    return pl.ds(pl.multiple_of(i * size, size), size)


def kernel(
    e_ref, f_ref, p_ref, l_ref, w_ref, gram_ref, new_ref,
    fl, fr, feat, featr, wpad, wown, wall, ts, tb, st, ulab, us, ub,
    gs, gr, gsum, gb16, ra, rb, cs, rc, xb, xt, gb,
    x_s, x_r, q_s, q_r, z_s, z_r, y_s, y_r, sl_s, sl_r, sr_s, sr_r,
    w_s, w_r, t_s, t_r, a_s, a_r, u_s, u_r, g_s, g_r, ra_s, ra_r, rb_s, rb_r, rc_s, rc_r,
    o_s, o_r, v_s,
):
    r, c, d = lax.axis_index("trow"), lax.axis_index("tcol"), lax.axis_index("dp")
    x, zl = lax.div(c, jnp.int32(2)), rem(c, 2)
    h, k = lax.div(d, jnp.int32(2)), rem(d, 2)
    sib = (r, c, 2 * h + 1 - k)
    mine = rows(k, HALF)
    sends = []

    def copy(src, dst, s, t, dev):
        return pltpu.make_async_remote_copy(
            src_ref=src, dst_ref=dst, send_sem=s, recv_sem=t, device_id=dev, device_id_type=MESH
        )

    def send(*args):
        m = copy(*args)
        m.start()
        sends.append(m)

    def arrived(ref, s, t):
        copy(ref, ref, s, t, sib).wait_recv()

    fl[c, :, :DIN] = f_ref[...].astype(F32).T.astype(BF16)
    ph = jnp.broadcast_to(p_ref[...], (W, W)).T
    hi = ph.astype(BF16)
    rest = ph - hi.astype(F32)
    mid = rest.astype(BF16)
    low = (rest - mid.astype(F32)).astype(BF16)
    lane = lax.broadcasted_iota(jnp.int32, (W, W), 1)
    packed = jnp.where(lane == 0, hi.astype(F32), 0.0)
    packed = jnp.where(lane == 1, mid.astype(F32), packed)
    packed = jnp.where(lane == 2, low.astype(F32), packed)
    fl[c, :, DIN:] = packed.astype(BF16)

    xp, xm = rem(x + 1, 4) * 2 + zl, rem(x + 3, 4) * 2 + zl
    xo = rem(x + 2, 4) * 2 + zl
    other = 1 - 2 * zl
    zdev = (r, c + other, 2 * rem(h + zl - k + 4, 4) + k)
    ydev = (rem(r + 7, N), c, d)
    half = fl.at[c, mine]
    send(half, half, x_s.at[0], x_r.at[0], (r, xp, d))
    send(half, half, x_s.at[1], x_r.at[1], (r, xm, d))
    send(half, fr.at[0, mine], y_s.at[0], y_r.at[0], ydev)
    send(half, half, z_s.at[0], z_r.at[0], zdev)

    wpad[...] = jnp.zeros_like(wpad)
    wpad[:, :CLS] = w_ref[...]
    wown[...] = wpad[...].T.astype(BF16)
    wcols = rows(place(d), W)

    def send_w(i, _):
        there = wall.at[:, wcols]

        @pl.when(jnp.logical_or(r != c, i != d))
        def _():
            copy(wown, there, w_s.at[i], w_r.at[d], (c, r, i)).start()

        return 0

    lax.fori_loop(0, N, send_w, 0)

    @pl.when(r == c)
    def _():
        wall[:, wcols] = wown[...]

    def features(src, store):
        phase = src[:, DIN:].astype(F32)
        phase = phase[:, 0:1] + phase[:, 1:2] + phase[:, 2:3]

        def part(i, _):
            s = rows(i, 256)
            angle = dot(src[:, :DIN], e_ref[s, :], NT) + phase
            t = angle * INV_PERIOD
            t = t - jnp.round(t)
            u = t * t
            v = jnp.full_like(u, COS[-1])
            for q in COS[-2::-1]:
                v = v * u + q
            store(s, v.astype(BF16))
            return 0

        lax.fori_loop(0, ROWS // 256, part, 0)

    def left(j):
        def store(s, v):
            feat[rows(place(j), W), s] = v

        features(fl.at[j], store)

    def right(i):
        def store(s, v):
            featr[i * W : (i + 1) * W, s] = v

        features(fr.at[i - 1], store)

    def to_sib_l(j, i):
        send(fl.at[j, mine], fl.at[j, mine], sl_s.at[i], sl_r.at[i], sib)

    def sib_l(j, i):
        arrived(fl.at[j, rows(1 - k, HALF)], sl_s.at[i], sl_r.at[i])

    def hop_y(i):
        piece = fr.at[i, mine]
        arrived(piece, y_s.at[i], y_r.at[i])
        if i < ND - 2:
            send(piece, fr.at[i + 1, mine], y_s.at[i + 1], y_r.at[i + 1], ydev)
        send(piece, piece, sr_s.at[i], sr_r.at[i], sib)

    def sib_r(i):
        arrived(fr.at[i, rows(1 - k, HALF)], sr_s.at[i], sr_r.at[i])

    left(c)
    featr[0:W, :] = feat[rows(place(c), W), :]

    quarters = (pl.ds(pl.multiple_of(k * HALF, 32), 32), pl.ds(pl.multiple_of(k * HALF + 32, 32), 32))
    for i, (j, on) in enumerate(((xm, xp), (xp, xm))):
        arrived(fl.at[j, mine], x_s.at[i], x_r.at[i])
        send(fl.at[j, quarters[i]], fl.at[j, quarters[i]], q_s.at[i], q_r.at[i], (r, on, d))
        send(fl.at[j, mine], fl.at[j, mine], z_s.at[1 + i], z_r.at[1 + i], zdev)
        to_sib_l(j, i)
    hop_y(0)
    zc = c + other
    arrived(fl.at[zc, mine], z_s.at[0], z_r.at[0])
    to_sib_l(zc, 2)
    for i in range(2):
        arrived(fl.at[xo, quarters[i]], q_s.at[i], q_r.at[i])
    send(fl.at[xo, mine], fl.at[xo, mine], z_s.at[3], z_r.at[3], zdev)
    to_sib_l(xo, 3)
    sib_l(xm, 0)
    left(xm)
    hop_y(1)
    sib_l(xp, 1)
    left(xp)
    for i, j in ((1, xm + other), (2, xp + other)):
        arrived(fl.at[j, mine], z_s.at[i], z_r.at[i])
        to_sib_l(j, 3 + i)
    sib_l(zc, 2)
    left(zc)
    hop_y(2)
    sib_l(xo, 3)
    left(xo)
    arrived(fl.at[xo + other, mine], z_s.at[3], z_r.at[3])
    to_sib_l(xo + other, 6)
    hop_y(3)
    for i, j in ((4, xm + other), (5, xp + other), (6, xo + other)):
        sib_l(j, i)
        left(j)

    def wait_w(i, _):
        @pl.when(jnp.logical_or(r != c, i != d))
        def _():
            arrived(wall.at[:, rows(place(i), W)], w_s.at[i], w_r.at[i])

        return 0

    lax.fori_loop(0, N, wait_w, 0)
    ts[...] = dot(wall[...], feat[...], NN).astype(BF16)

    def send_t(i, _):
        @pl.when(i != r)
        def _():
            copy(ts.at[rows(i, 16)], tb.at[r], t_s.at[i], t_r.at[r], (i, c, d)).start()

        return 0

    lax.fori_loop(0, N, send_t, 0)
    tb[r] = ts[rows(r, 16), :]

    for i in range(1, ND):
        sib_r(i - 1)
        right(i)

    scale = 1.0 / TOTAL
    gs[...] = (dot(feat[rows(1 - k, 512), :], featr[...], NT) * scale).astype(BF16)
    send(gs, gr, g_s.at[0], g_r.at[0], sib)
    gsum[...] = dot(feat[rows(k, 512), :], featr[...], NT) * scale

    def wait_t(i, _):
        @pl.when(i != r)
        def _():
            arrived(tb.at[i], t_s.at[i], t_r.at[i])

        return 0

    lax.fori_loop(0, N, wait_t, 0)
    total = tb[0].astype(F32)
    for i in range(1, N):
        total = total + tb[i].astype(F32)
    st[rows(r, 16), :] = total.astype(BF16)

    def send_a(i, _):
        @pl.when(i != r)
        def _():
            copy(st.at[rows(r, 16)], st.at[rows(r, 16)], a_s.at[i], a_r.at[r], (i, c, d)).start()

        return 0

    lax.fori_loop(0, N, send_a, 0)

    arrived(gr, g_s.at[0], g_r.at[0])
    gsum[...] = gsum[...] + gr[...].astype(F32)
    gb16[...] = gsum[...].astype(BF16)
    hp, hm, ho = rem(h + 1, 4), rem(h + 3, 4), rem(h + 2, 4)
    up, down = (r, c, 2 * hp + k), (r, c, 2 * hm + k)

    def part(i, half):
        return pl.ds(pl.multiple_of(i * W + half * HALF, HALF), HALF)

    send(gb16.at[part(ho, 0)], ra.at[0], ra_s.at[0], ra_r.at[0], up)
    send(gb16.at[part(ho, 1)], ra.at[1], ra_s.at[1], ra_r.at[1], down)
    send(gb16.at[part(hp, 1)], rb.at[0], rb_s.at[0], rb_r.at[0], up)
    send(gb16.at[part(hm, 0)], rb.at[1], rb_s.at[1], rb_r.at[1], down)

    cls = lax.broadcasted_iota(jnp.int32, (W, ROWS), 0)
    onehot = jnp.where(l_ref[...] == cls + c * CLS, 1.0, 0.0).astype(BF16)
    own_f = feat[...].astype(F32)
    diag = jnp.sum(own_f * own_f, axis=1, keepdims=True)
    lane_u = lax.broadcasted_iota(jnp.int32, (N * W, W), 1)
    ulab[...] = jnp.where(lane_u == CLS, diag, -C * dot(feat[...], onehot, NT)) * scale

    for i, (to, dev) in enumerate(((hp, up), (hm, down))):
        arrived(ra.at[i], ra_s.at[i], ra_r.at[i])
        cs[i] = (gsum[part(to, i), :] + ra[i].astype(F32)).astype(BF16)
        send(cs.at[i], rc.at[i], rc_s.at[i], rc_r.at[i], dev)

    def wait_a(i, _):
        @pl.when(i != r)
        def _():
            arrived(st.at[rows(i, 16)], a_s.at[i], a_r.at[i])

        return 0

    lax.fori_loop(0, N, wait_a, 0)
    step = dot(feat[...], st[...], NT) * scale
    us[...] = (jnp.where(lane_u == CLS, 0.0, step) + ulab[...]).astype(BF16)

    def send_u(i, _):
        @pl.when(jnp.logical_or(r != c, i != d))
        def _():
            copy(us.at[rows(place(i), W)], ub.at[d], u_s.at[i], u_r.at[d], (c, r, i)).start()

        return 0

    lax.fori_loop(0, N, send_u, 0)

    @pl.when(r == c)
    def _():
        ub[d] = us[rows(place(d), W), :]

    for i in range(2):
        arrived(rb.at[i], rb_s.at[i], rb_r.at[i])
        arrived(rc.at[i], rc_s.at[i], rc_r.at[i])
    top = gsum[part(h, 0), :] + rc[0].astype(F32) + rb[1].astype(F32)
    low_half = gsum[part(h, 1), :] + rb[0].astype(F32) + rc[1].astype(F32)
    total = jnp.concatenate([top, low_half], axis=0)
    for i in range(ND):
        xb[i] = total[:, i * W : (i + 1) * W].astype(BF16)
        to = rem(r + i, N)

        @pl.when(to != c)
        def _():
            copy(xb.at[i], gb.at[c], o_s.at[i], o_r.at[c], (r, to, d)).start()

        @pl.when(to == c)
        def _():
            gb[c] = xb[i]

        if 0 < i < ND - 1:
            xt[i - 1] = total[:, i * W : (i + 1) * W].T.astype(BF16)
            send(xt.at[i - 1], gb.at[d], v_s.at[i - 1], o_r.at[d], (to, r, c))

    def wait_u(i, _):
        @pl.when(jnp.logical_or(r != c, i != d))
        def _():
            arrived(ub.at[i], u_s.at[i], u_r.at[i])

        return 0

    lax.fori_loop(0, N, wait_u, 0)
    grad = ub[0].astype(F32)
    for i in range(1, N):
        grad = grad + ub[i].astype(F32)
    old = wpad[...]
    diag = grad[:, CLS : CLS + 1] + RIDGE
    new = old - STEP_RATE * (grad + RIDGE * old) / diag
    new_ref[...] = new[:, :CLS]

    delta = rem(c - r + N, N)

    def wait_o(i, _):
        @pl.when(jnp.logical_or(delta >= ND, i != c))
        def _():
            arrived(gb.at[i], o_s.at[0], o_r.at[i])

        return 0

    lax.fori_loop(0, N, wait_o, 0)
    eye = lax.broadcasted_iota(jnp.int32, (W, W), 0) == lane
    for i in range(N):
        ridge = jnp.where(jnp.logical_and(eye, jnp.logical_and(r == c, d == i)), RIDGE, 0.0)
        gram_ref[:, i * W : (i + 1) * W] = gb[i].astype(F32) + ridge

    for m in sends:
        m.wait_send()

    def sent(i, _):
        @pl.when(jnp.logical_or(r != c, i != d))
        def _():
            copy(wown, wown, w_s.at[i], w_r.at[i], sib).wait_send()
            copy(ub.at[0], ub.at[0], u_s.at[i], u_r.at[i], sib).wait_send()

        @pl.when(i != r)
        def _():
            copy(tb.at[0], tb.at[0], t_s.at[i], t_r.at[i], sib).wait_send()
            copy(tb.at[0], tb.at[0], a_s.at[i], a_r.at[i], sib).wait_send()

        return 0

    lax.fori_loop(0, N, sent, 0)
    for i in range(ND):

        @pl.when(rem(r + i, N) != c)
        def _():
            copy(xb.at[i], xb.at[i], o_s.at[i], o_r.at[0], sib).wait_send()


def shards(embeds, frequencies, phases, labels, weights):
    vmem = pl.BlockSpec(memory_space=pltpu.VMEM)
    sem = lambda *n: pltpu.SemaphoreType.DMA(n)
    buffers = [
        ((N, W, WIDE), BF16),
        ((ND - 1, W, WIDE), BF16),
        ((N * W, ROWS), BF16),
        ((ND * W, ROWS), BF16),
        ((W, W), F32),
        ((W, W), BF16),
        ((W, N * W), BF16),
        ((W, ROWS), BF16),
        ((N, 16, ROWS), BF16),
        ((W, ROWS), BF16),
        ((N * W, W), F32),
        ((N * W, W), BF16),
        ((N, W, W), BF16),
        ((4 * W, ND * W), BF16),
        ((4 * W, ND * W), BF16),
        ((4 * W, ND * W), F32),
        ((4 * W, ND * W), BF16),
        ((2, HALF, ND * W), BF16),
        ((2, HALF, ND * W), BF16),
        ((2, HALF, ND * W), BF16),
        ((2, HALF, ND * W), BF16),
        ((ND, W, W), BF16),
        ((ND - 2, W, W), BF16),
        ((N, W, W), BF16),
    ]
    pairs = [2, 2, 4, 4, 7, 4, N, N, N, N, 1, 2, 2, 2]
    sems = [sem(n) for n in pairs for _ in range(2)] + [sem(ND), sem(N), sem(ND - 2)]
    return pl.pallas_call(
        kernel,
        out_shape=(
            jax.ShapeDtypeStruct((W, N * W), F32),
            jax.ShapeDtypeStruct((W, CLS), F32),
        ),
        in_specs=[vmem] * 5,
        out_specs=(vmem, vmem),
        scratch_shapes=[pltpu.VMEM(*b) for b in buffers] + sems,
        compiler_params=pltpu.CompilerParams(
            has_side_effects=True, vmem_limit_bytes=50 * 2**20
        ),
    )(embeds, frequencies, phases.reshape(1, W), labels.reshape(1, ROWS), weights)


def solution(mesh):
    return jax.shard_map(
        shards,
        mesh=mesh,
        in_specs=(
            P("dp", None),
            P(None, ("trow", "tcol")),
            P(("trow", "tcol")),
            P("dp"),
            P(("tcol", "dp"), "trow"),
        ),
        out_specs=(P(("trow", "dp"), "tcol"), P(("tcol", "dp"), "trow")),
        check_vma=False,
    )
```

time: 349 us -> 150 us (0.43)
  waiting for transfers between devices: 228 us -> 0 us
  Pallas kernels: 0 us -> 140 us
  blocking collectives: 41.7 us -> 0 us
  matrix products: 18.6 us -> 0 us
  between operations: 15.4 us -> 0.65 us
  local copies, waits for them, and re-layouts: 20.1 us -> 6.14 us
  starting transfers between devices: 12.4 us -> 0 us
  other arithmetic: 8.31 us -> 0 us
    pallas_call x0 -> x1, Pallas kernels: none -> 140 us  [shards(): pl.pallas_call(kernel, out_shape=(jax.ShapeDtypeStruct((W, N * W), F32),...]
    all_gather x3 -> x0, waiting for transfers between devices: 101 us -> none  [the longest x1 50.1 us: broadcast_by_parts(): lax.all_gather(own, axis, axis=0, tiled=True)[:len(lines)]]
    unnamed x6 -> x0, waiting for transfers between devices: 47.3 us -> none
    reduce_scatter x1 -> x0, waiting for transfers between devices: 46.7 us -> none  [shards(): lax.psum_scatter((lax.dot_general(left_feats, right_feats, contract, pref...]
    all_to_all x2 -> x0, waiting for transfers between devices: 33 us -> none  [the longest x1 22.6 us: copy_for_each(): lax.all_to_all(jnp.broadcast_to(array[None], (size, *array.shape)), axis,...]
    all_to_all x1 -> x0, blocking collectives: 29.7 us -> none  [copy_for_each(): lax.all_to_all(jnp.broadcast_to(array[None], (size, *array.shape)), axis,...]
    dot_general x5 -> x0, matrix products: 18.6 us -> none  [the longest x1 5.91 us: shards(): lax.dot_general(left_feats, right_feats, contract, preferred_element_type...]
    all_to_all x2 -> x0, starting transfers between devices: 12.2 us -> none  [the longest x1 6.66 us: copy_for_each(): lax.all_to_all(jnp.broadcast_to(array[None], (size, *array.shape)), axis,...]
  transfers between devices with their start and end apart: 7 -> 0, of which waited for: 7 -> 0; matrix products, arithmetic and copies ran while one was open for 2% -> 0% of each run, Pallas kernels for 0% -> 0%
where the time goes in v1:
time: 150 us; the launch traced here: 147 us
  Pallas kernels  140 us (93%)
  local copies, waits for them, and re-layouts  6.14 us (4%)
    pallas_call x1, Pallas kernels, shards(): pl.pallas_call(kernel, out_shape=(jax.ShapeDtypeStruct((W, N * W), F32),...  140 us
    unnamed x12, local copies, waits for them, and re-layouts  6.14 us

profile of v1, /device:TPU:1, one launch (start us, length us, event | category | flops | bytes accessed | tf_op | source)
XLA Modules:
  0.0 147.0 jit_solution(14781197632882114280)
XLA Ops:
  0.6 0.0 copy-start
  0.6 1.6 %copy-done = bf16[1024,1024]{1,0:T(8,128)(2,1)S(1)} copy-done((bf16[1024,1024]{1,0:T(8,128)(2,1)S(1)}, bf16[1024,1024]{1,0:T(8,128)(2,1)}, u32[]{:S(2)}) %copy-start) | copy-done | bytes 2097176
  2.2 0.0 copy-start.1
  2.2 0.9 copy-done.1
  3.2 0.0 copy-start.2
  3.2 0.8 copy-done.2
  4.0 0.0 copy-start.3
  4.0 0.7 copy-done.3
  4.7 0.0 copy-start.4
  4.7 0.7 copy-done.4
  5.4 140.2 %shard_map.68 = (f32[128,1024]{1,0:T(8,128)S(1)}, f32[128,125]{1,0:T(8,128)S(1)}) custom-call(bf16[1024,1024]{1,0:T(8,128)(2,1)S(1)} %copy-done, bf16[1024,128]{1,0:T(8,128)(2,1)S(1)} %copy-done.1, f32[1,128]{1,0:T(1,128)S(1)} %bitcast.3, s32[1,1024]{1,0:T(1,128)S(1)} %bitcast.2, f32[128,125]{1,0:T(8,128)S(1)} %copy-done.2), custom_call_target="tpu_custom_call" | custom-call | tf_op jit(solution)/shard_map/pallas_call | solution.py:419
  145.5 0.8 copy.9
  146.3 0.6 copy.10
Async XLA Ops:
  0.6 1.6 %copy-start = (bf16[1024,1024]{1,0:T(8,128)(2,1)S(1)}, bf16[1024,1024]{1,0:T(8,128)(2,1)}, u32[]{:S(2)}) copy-start(bf16[1024,1024]{1,0:T(8,128)(2,1)} %e_ref.1) | copy-start | bytes 6291460
  2.2 0.9 copy-start.1
  3.2 0.8 copy-start.2
  4.0 0.7 copy-start.3
  4.7 0.7 copy-start.4

commit v2 on v1

v2 whole, which is shorter than its diff:
```python
import jax
import jax.numpy as jnp
from jax import lax
from jax.experimental import pallas as pl
from jax.experimental.pallas import tpu as pltpu
from jax.sharding import PartitionSpec as P

C = 1000
RIDGE = 0.5
STEP_RATE = 0.5
MESH = pl.DeviceIdType.MESH
F32, BF16 = jnp.float32, jnp.bfloat16
NT = (((1,), (1,)), ((), ()))
NN = (((1,), (0,)), ((), ()))

N = 8
W = 128
ROWS = 1024
DIN = 1024
WIDE = DIN + 128
HALF = W // 2
CLS = 125
TOTAL = 8192
ND = 5
GROUPS = (3 * W, 2 * W, W)
INV_PERIOD = 0.15915494309189535
COS = [
    1.4142135623730951 * q
    for q in (
        0.9999999890754399,
        -19.73920450099313,
        64.93911749956553,
        -85.45013994347214,
        60.16763282514798,
        -25.967602441408868,
        6.528658639370483,
    )
]


def dot(a, b, dims):
    return lax.dot_general(a, b, dims, preferred_element_type=F32)


def rem(a, b):
    return lax.rem(a, jnp.int32(b))


def place(a):
    return rem(a, 2) * 4 + lax.div(a, jnp.int32(2))


def rows(i, size):
    return pl.ds(pl.multiple_of(i * size, size), size)


def kernel(
    e_hbm, f_hbm, p_hbm, l_hbm, w_hbm, gram_hbm, new_hbm,
    e_ref, f_ref, p_ref, l_ref, w_ref, gram_ref, new_ref,
    fl, fr, feat, featr, wpad, wown, wall, ts, tb, st, ulab, xb, xt, gb, us, ub, *rest
):
    kinds = ("gs", "gr", "gsum", "gb16", "ra", "rb", "cs", "rc", "sem_s", "sem_r")
    groups = [dict(zip(kinds, rest[i :: len(GROUPS)])) for i in range(len(GROUPS))]
    (
        in_s, out_s, x_s, x_r, q_s, q_r, z_s, z_r, y_s, y_r, sl_s, sl_r, sr_s, sr_r,
        w1_s, w1_r, w2_s, w2_r, w3_s, w3_r, t_s, t_r, a_s, a_r, u_s, u_r, o_s, o_r, v_s,
    ) = rest[len(kinds) * len(GROUPS) :]
    r, c, d = lax.axis_index("trow"), lax.axis_index("tcol"), lax.axis_index("dp")
    x, zl = lax.div(c, jnp.int32(2)), rem(c, 2)
    h, k = lax.div(d, jnp.int32(2)), rem(d, 2)
    other = 1 - 2 * zl
    sib = (r, c, 2 * h + 1 - k)
    flipped = (c, r, d)
    zdev = (r, c + other, 2 * rem(h + zl - k + 4, 4) + k)
    zsrc = (r, c + other, 2 * rem(h + zl + k + 3, 4) + k)
    sends = []

    barrier = pltpu.get_barrier_semaphore()

    def here(*dev):
        pl.semaphore_signal(barrier, inc=1, device_id=dev, device_id_type=MESH)

    def greet(i, _):
        here(rem(r + i, N), c, d)
        here(r, rem(c + i, N), d)
        here(r, c, rem(d + i, N))
        return 0

    lax.fori_loop(1, N, greet, 0)
    here(*zsrc)

    @pl.when(r != c)
    def _():
        here(*flipped)

    behind = rem(r - c + N, N)

    @pl.when(jnp.logical_and(behind >= 1, behind <= ND - 2))
    def _():
        def to_source(i, _):
            here(c, d, i)
            return 0

        lax.fori_loop(0, N, to_source, 0)

    loads = [
        pltpu.make_async_copy(a, b, in_s.at[i])
        for i, (a, b) in enumerate(
            ((f_hbm, f_ref), (p_hbm, p_ref), (w_hbm, w_ref), (l_hbm, l_ref), (e_hbm, e_ref))
        )
    ]
    for m in loads:
        m.start()

    def copy(src, dst, s, t, dev):
        return pltpu.make_async_remote_copy(
            src_ref=src, dst_ref=dst, send_sem=s, recv_sem=t, device_id=dev, device_id_type=MESH
        )

    def send(*args):
        m = copy(*args)
        m.start()
        sends.append(m)

    def arrived(ref, s, t):
        copy(ref, ref, s, t, sib).wait_recv()

    def half(i, core=None):
        return pl.ds(pl.multiple_of(i * W + (k if core is None else core) * HALF, HALF), HALF)

    lane = lax.broadcasted_iota(jnp.int32, (W, W), 1)
    loads[0].wait()
    fl[:W, :DIN] = f_ref[...].astype(F32).T.astype(BF16)
    loads[1].wait()
    ph = jnp.broadcast_to(p_ref[...], (W, W)).T
    hi = ph.astype(BF16)
    left_over = ph - hi.astype(F32)
    mid = left_over.astype(BF16)
    low = (left_over - mid.astype(F32)).astype(BF16)
    packed = jnp.where(lane == 0, hi.astype(F32), 0.0)
    packed = jnp.where(lane == 1, mid.astype(F32), packed)
    packed = jnp.where(lane == 2, low.astype(F32), packed)
    fl[:W, DIN:] = packed.astype(BF16)
    loads[2].wait()
    wpad[...] = jnp.zeros_like(wpad)
    wpad[:, :CLS] = w_ref[...]
    wown[...] = wpad[...].T.astype(BF16)

    pl.semaphore_wait(barrier, 3 * (N - 1) + 1 + ND - 2 + jnp.where(r != c, 1, 0))

    xp, xm, xo = (rem(x + i, 4) * 2 + zl for i in (1, 3, 2))
    slots = [c, xm, xp, xo, c + other, xm + other, xp + other, xo + other]
    ydev = (rem(r + 7, N), c, d)
    own = fl.at[half(0)]
    send(own, fl.at[half(1)], x_s.at[0], x_r.at[0], (r, xp, d))
    send(own, fl.at[half(2)], x_s.at[1], x_r.at[1], (r, xm, d))
    send(own, fr.at[half(0)], y_s.at[0], y_r.at[0], ydev)
    send(own, fl.at[half(4)], z_s.at[0], z_r.at[0], zdev)

    wcols = rows(place(d), W)
    wmine = wall.at[:, wcols]

    @pl.when(r != c)
    def _():
        copy(wown, wmine, w1_s.at[0], w1_r.at[0], flipped).start()

    @pl.when(r == c)
    def _():
        wall[:, wcols] = wown[...]

    def cosines(src, n):
        phase = src[:, DIN:].astype(F32)
        phase = phase[:, 0:1] + phase[:, 1:2] + phase[:, 2:3]
        angle = dot(src[:, :DIN], e_ref[...], NT) + phase
        t = angle * INV_PERIOD
        t = t - jnp.round(t)
        u = t * t
        v = jnp.full_like(u, COS[-1])
        for q in COS[-2::-1]:
            v = v * u + q
        return v.astype(BF16)

    def left(first, n):
        v = cosines(fl.at[first * W : (first + n) * W], n)
        for i in range(n):
            feat[rows(place(slots[first + i]), W), :] = v[i * W : (i + 1) * W]

    def right(first, n):
        featr[(first + 1) * W : (first + 1 + n) * W, :] = cosines(fr.at[first * W : (first + n) * W], n)

    def to_sib(i):
        send(fl.at[half(i)], fl.at[half(i)], sl_s.at[i], sl_r.at[i], sib)

    def to_z(i):
        send(fl.at[half(i)], fl.at[half(4 + i)], z_s.at[i], z_r.at[i], zdev)

    def from_z(i):
        arrived(fl.at[half(4 + i)], z_s.at[i], z_r.at[i])
        to_sib(4 + i)

    def from_sib(*which):
        for i in which:
            arrived(fl.at[half(i, 1 - k)], sl_s.at[i], sl_r.at[i])

    def hop_y(i):
        piece = fr.at[half(i)]
        arrived(piece, y_s.at[i], y_r.at[i])
        if i < ND - 2:
            send(piece, fr.at[half(i + 1)], y_s.at[i + 1], y_r.at[i + 1], ydev)
        send(piece, piece, sr_s.at[i], sr_r.at[i], sib)

    def sib_y(*which):
        for i in which:
            arrived(fr.at[half(i, 1 - k)], sr_s.at[i], sr_r.at[i])

    loads[4].wait()
    left(0, 1)
    featr[0:W, :] = feat[rows(place(c), W), :]

    def quarter(slot, i):
        return fl.at[pl.ds(pl.multiple_of(slot * W + k * HALF + i * 32, 32), 32)]

    for i, (slot, on) in enumerate(((1, xp), (2, xm))):
        arrived(fl.at[half(slot)], x_s.at[i], x_r.at[i])
        send(quarter(slot, i), quarter(3, i), q_s.at[i], q_r.at[i], (r, on, d))
        to_z(slot)
        to_sib(slot)
    hop_y(0)
    from_z(0)

    @pl.when(r != c)
    def _():
        arrived(wmine, w1_s.at[0], w1_r.at[0])

    send(wmine, wmine, w3_s.at[0], w3_r.at[0], sib)
    for i in range(1, 4):
        send(wmine, wmine, w2_s.at[i], w2_r.at[i], (r, c, 2 * rem(h + i, 4) + k))

    from_sib(1, 2)
    left(1, 2)
    hop_y(1)
    for i in range(2):
        arrived(quarter(3, i), q_s.at[i], q_r.at[i])
    to_z(3)
    to_sib(3)
    from_z(1)
    from_z(2)
    for i in range(1, 4):
        piece = wall.at[:, rows(place(2 * rem(h + 4 - i, 4) + k), W)]
        arrived(piece, w2_s.at[i], w2_r.at[i])
        send(piece, piece, w3_s.at[i], w3_r.at[i], sib)
    from_sib(3, 4)
    left(3, 2)
    hop_y(2)
    from_z(3)
    from_sib(5, 6, 7)
    left(5, 3)

    for i in range(4):
        arrived(wall.at[:, rows(place(2 * rem(h + 4 - i, 4) + 1 - k), W)], w3_s.at[i], w3_r.at[i])
    ts[...] = dot(wall[...], feat[...], NN).astype(BF16)
    for i in range(1, N):
        to = rem(r + i, N)
        send(ts.at[rows(to, 16)], tb.at[i], t_s.at[i], t_r.at[i], (to, c, d))
    hop_y(3)

    scale = 1.0 / TOTAL

    def gram_partial(g, first, n):
        cols = featr[first * W : (first + n) * W, :]
        g["gs"][...] = (dot(feat[rows(1 - k, 512), :], cols, NT) * scale).astype(BF16)
        swap(g)
        g["gsum"][...] = dot(feat[rows(k, 512), :], cols, NT) * scale

    def swap(g):
        send(g["gs"], g["gr"], g["sem_s"].at[0], g["sem_r"].at[0], sib)

    hp, hm, ho = rem(h + 1, 4), rem(h + 3, 4), rem(h + 2, 4)
    up, down = (r, c, 2 * hp + k), (r, c, 2 * hm + k)

    def step_one(g):
        arrived(g["gr"], g["sem_s"].at[0], g["sem_r"].at[0])
        g["gsum"][...] = g["gsum"][...] + g["gr"][...].astype(F32)
        g["gb16"][...] = g["gsum"][...].astype(BF16)
        for n, (name, i, at, core, dev) in enumerate(
            (
                ("ra", 0, ho, 0, up),
                ("ra", 1, ho, 1, down),
                ("rb", 0, hp, 1, up),
                ("rb", 1, hm, 0, down),
            )
        ):
            send(g["gb16"].at[half(at, core)], g[name].at[i], g["sem_s"].at[1 + n], g["sem_r"].at[1 + n], dev)

    def step_two(g):
        for i, (at, dev) in enumerate(((hp, up), (hm, down))):
            arrived(g["ra"].at[i], g["sem_s"].at[1 + i], g["sem_r"].at[1 + i])
            g["cs"][i] = (g["gsum"][half(at, i), :] + g["ra"][i].astype(F32)).astype(BF16)
            send(g["cs"].at[i], g["rc"].at[i], g["sem_s"].at[5 + i], g["sem_r"].at[5 + i], dev)

    def step_three(g):
        for i in range(2):
            arrived(g["rb"].at[i], g["sem_s"].at[3 + i], g["sem_r"].at[3 + i])
            arrived(g["rc"].at[i], g["sem_s"].at[5 + i], g["sem_r"].at[5 + i])
        upper = g["gsum"][half(h, 0), :] + g["rc"][0].astype(F32) + g["rb"][1].astype(F32)
        lower = g["gsum"][half(h, 1), :] + g["rb"][0].astype(F32) + g["rc"][1].astype(F32)
        return jnp.concatenate([upper, lower], axis=0)

    def hand_out(g, first, n):
        total = step_three(g)
        for i in range(first, first + n):
            block = total[:, (i - first) * W : (i - first + 1) * W]
            xb[i] = block.astype(BF16)
            to = rem(r + i, N)

            @pl.when(to != c)
            def _():
                copy(xb.at[i], gb.at[c], o_s.at[i], o_r.at[c], (r, to, d)).start()

            @pl.when(to == c)
            def _():
                gb[c] = xb[i]

            if 0 < i < ND - 1:
                xt[i - 1] = block.T.astype(BF16)
                send(xt.at[i - 1], gb.at[d], v_s.at[i - 1], o_r.at[d], (to, r, c))

    sib_y(0, 1)
    right(0, 2)
    gram_partial(groups[0], 0, 3)
    step_one(groups[0])

    total = ts[rows(r, 16), :].astype(F32)
    for i in range(1, N):
        arrived(tb.at[i], t_s.at[i], t_r.at[i])
        total = total + tb[i].astype(F32)
    strip = st.at[rows(r, 16)]
    st[rows(r, 16), :] = total.astype(BF16)
    for i in range(1, N):
        send(strip, strip, a_s.at[i], a_r.at[i], (rem(r + i, N), c, d))

    sib_y(2, 3)
    right(2, 2)
    step_two(groups[0])
    gram_partial(groups[1], 3, 2)
    step_one(groups[1])

    loads[3].wait()
    cls = lax.broadcasted_iota(jnp.int32, (W, ROWS), 0)
    onehot = jnp.where(l_ref[...] == cls + c * CLS, 1.0, 0.0).astype(BF16)
    own_f = feat[...].astype(F32)
    diag = jnp.sum(own_f * own_f, axis=1, keepdims=True)
    lane_u = lax.broadcasted_iota(jnp.int32, (N * W, W), 1)
    ulab[...] = jnp.where(lane_u == CLS, diag, -C * dot(feat[...], onehot, NT)) * scale
    hand_out(groups[0], 0, 3)
    step_two(groups[1])

    for i in range(1, N):
        arrived(st.at[rows(rem(r + N - i, N), 16)], a_s.at[i], a_r.at[i])
    ulab[...] = jnp.where(lane_u == CLS, 0.0, dot(feat[...], st[...], NT) * scale) + ulab[...]
    g = groups[2]
    g["gs"][...] = ulab[rows(1 - k, 512), :].astype(BF16)
    swap(g)
    g["gsum"][...] = ulab[rows(k, 512), :]
    step_one(g)
    hand_out(groups[1], 3, 2)
    step_two(g)

    delta = rem(c - r + N, N)
    eye = lax.broadcasted_iota(jnp.int32, (W, W), 0) == lane

    def gram_block(i, _):
        @pl.when(jnp.logical_or(delta >= ND, i != c))
        def _():
            arrived(gb.at[i], o_s.at[0], o_r.at[i])

        ridge = jnp.where(jnp.logical_and(eye, jnp.logical_and(r == c, d == i)), RIDGE, 0.0)
        gram_ref[i] = gb[i].astype(F32) + ridge
        pltpu.make_async_copy(gram_ref.at[i], gram_hbm.at[:, rows(i, W)], out_s.at[i]).start()
        return 0

    total = step_three(g)
    first = total.astype(BF16).astype(F32)
    second = (total - first)[:, CLS : CLS + 1]
    us[...] = jnp.where(lane == CLS + 1, second, total).astype(BF16)

    @pl.when(r != c)
    def _():
        copy(us, ub, u_s.at[0], u_r.at[0], flipped).start()

    @pl.when(r == c)
    def _():
        ub[...] = us[...]

    lax.fori_loop(0, N, gram_block, 0)

    @pl.when(r != c)
    def _():
        arrived(ub, u_s.at[0], u_r.at[0])

    grad = ub[...].astype(F32)
    old = wpad[...]
    diag = grad[:, CLS : CLS + 1] + grad[:, CLS + 1 : CLS + 2] + RIDGE
    new = old - STEP_RATE * (grad + RIDGE * old) / diag
    new_ref[...] = new[:, :CLS]
    last = pltpu.make_async_copy(new_ref, new_hbm, out_s.at[N])
    last.start()

    for m in sends:
        m.wait_send()

    @pl.when(r != c)
    def _():
        copy(wown, wown, w1_s.at[0], w1_r.at[0], sib).wait_send()
        copy(us, us, u_s.at[0], u_r.at[0], sib).wait_send()

    for i in range(ND):

        @pl.when(rem(r + i, N) != c)
        def _():
            copy(xb.at[i], xb.at[i], o_s.at[i], o_r.at[0], sib).wait_send()

    def written(i, _):
        pltpu.make_async_copy(gram_ref.at[i], gram_hbm.at[:, rows(i, W)], out_s.at[i]).wait()
        return 0

    lax.fori_loop(0, N, written, 0)
    last.wait()


def shards(embeds, frequencies, phases, labels, weights):
    hbm = pl.BlockSpec(memory_space=pl.ANY)
    buffers = [
        ((ROWS, DIN), BF16),
        ((DIN, W), BF16),
        ((1, W), F32),
        ((1, ROWS), jnp.int32),
        ((W, CLS), F32),
        ((N, W, W), F32),
        ((W, CLS), F32),
        ((N * W, WIDE), BF16),
        (((ND - 1) * W, WIDE), BF16),
        ((N * W, ROWS), BF16),
        ((ND * W, ROWS), BF16),
        ((W, W), F32),
        ((W, W), BF16),
        ((W, N * W), BF16),
        ((W, ROWS), BF16),
        ((N, 16, ROWS), BF16),
        ((W, ROWS), BF16),
        ((N * W, W), F32),
        ((ND, W, W), BF16),
        ((ND - 2, W, W), BF16),
        ((N, W, W), BF16),
        ((W, W), BF16),
        ((W, W), BF16),
    ]
    for dtype in (BF16, BF16, F32, BF16):
        buffers += [((4 * W, n), dtype) for n in GROUPS]
    for _ in range(4):
        buffers += [((2, HALF, n), BF16) for n in GROUPS]
    sem = lambda n: pltpu.SemaphoreType.DMA((n,))
    sems = [sem(7)] * (2 * len(GROUPS)) + [sem(5), sem(N + 1)]
    for n in (2, 2, 4, 4, N, 4, 1, 4, 4, N, N, 1):
        sems += [sem(n), sem(n)]
    sems += [sem(ND), sem(N), sem(ND - 2)]
    return pl.pallas_call(
        kernel,
        out_shape=(
            jax.ShapeDtypeStruct((W, N * W), F32),
            jax.ShapeDtypeStruct((W, CLS), F32),
        ),
        in_specs=[hbm] * 5,
        out_specs=(hbm, hbm),
        scratch_shapes=[pltpu.VMEM(*b) for b in buffers] + sems,
        compiler_params=pltpu.CompilerParams(
            collective_id=0, has_side_effects=True, vmem_limit_bytes=56 * 2**20
        ),
    )(embeds, frequencies, phases.reshape(1, W), labels.reshape(1, ROWS), weights)


def solution(mesh):
    return jax.shard_map(
        shards,
        mesh=mesh,
        in_specs=(
            P("dp", None),
            P(None, ("trow", "tcol")),
            P(("trow", "tcol")),
            P("dp"),
            P(("tcol", "dp"), "trow"),
        ),
        out_specs=(P(("trow", "dp"), "tcol"), P(("tcol", "dp"), "trow")),
        check_vma=False,
    )
```

time: 150 us -> 79 us (0.53)
  the two profiles are of different devices: /device:TPU:1 before, /device:TPU:22 now
where the time goes in v2:
time: 79 us; the launch traced here: 78.7 us
  Pallas kernels  74.7 us (95%)
  local copies, waits for them, and re-layouts  3.36 us (4%)
    pallas_call x1, Pallas kernels, shards(): pl.pallas_call(kernel, out_shape=(jax.ShapeDtypeStruct((W, N * W), F32),...  74.7 us
    unnamed x2, local copies, waits for them, and re-layouts  3.36 us

profile of v2, /device:TPU:22, one launch (start us, length us, event | category | flops | bytes accessed | tf_op | source)
XLA Modules:
  0.0 78.7 jit_solution(6679146767244291536)
XLA Ops:
  0.6 74.7 %shard_map.68 = (f32[128,1024]{1,0:T(8,128)}, f32[128,125]{1,0:T(8,128)}) custom-call(bf16[1024,1024]{1,0:T(8,128)(2,1)} %e_hbm.1, bf16[1024,128]{1,0:T(8,128)(2,1)} %f_hbm.1, f32[1,128]{1,0:T(1,128)} %bitcast.3, s32[1,1024]{1,0:T(1,128)} %bitcast.2, f32[128,125]{1,0:T(8,128)} %w_hbm.1), custom_call_target="tpu_custom_call" | custom-call | tf_op jit(solution)/shard_map/pallas_call | solution.py:467
  75.4 1.9 %copy.9 = f32[128,1024]{1,0:T(8,128)} copy(f32[128,1024]{1,0:T(8,128)} %get-tuple-element.4) | data formatting | bytes 1048576
  77.3 1.5 %copy.10 = f32[128,125]{1,0:T(8,128)} copy(f32[128,125]{1,0:T(8,128)} %get-tuple-element.5) | data formatting | bytes 128000

commit v3 on v2

--- a/solution.py
+++ b/solution.py
@@ -17,25 +17,21 @@
 W = 128
 ROWS = 1024
 DIN = 1024
-WIDE = DIN + 128
 HALF = W // 2
 CLS = 125
 TOTAL = 8192
 ND = 5
 GROUPS = (3 * W, 2 * W, W)
 INV_PERIOD = 0.15915494309189535
-COS = [
+SIN = [
     1.4142135623730951 * q
     for q in (
-        0.9999999890754399,
-        -19.73920450099313,
-        64.93911749956553,
-        -85.45013994347214,
-        60.16763282514798,
-        -25.967602441408868,
-        6.528658639370483,
-    )
-]
+        6.283185160087748,
+        -41.34165503097383,
+        81.60100404358543,
+        -76.54978157108546,
+        39.53670029211564,
+    )]
 
 
 def dot(a, b, dims):
@@ -55,15 +51,15 @@
 
 
 def kernel(
-    e_hbm, f_hbm, p_hbm, l_hbm, w_hbm, gram_hbm, new_hbm,
-    e_ref, f_ref, p_ref, l_ref, w_ref, gram_ref, new_ref,
-    fl, fr, feat, featr, wpad, wown, wall, ts, tb, st, ulab, xb, xt, gb, us, ub, *rest
+    e_hbm, f_hbm, p_hbm, l_hbm, w_hbm, gram_ref, new_ref,
+    e_ref, f_ref, p_ref, l_ref, w_ref, pall, prow, pcol,
+    fl, fr, feat, featr, wpad, wown, wall, ts, tb, st, ulab, xb, xt, xr, gb, us, ub, *rest
 ):
     kinds = ("gs", "gr", "gsum", "gb16", "ra", "rb", "cs", "rc", "sem_s", "sem_r")
     groups = [dict(zip(kinds, rest[i :: len(GROUPS)])) for i in range(len(GROUPS))]
     (
-        in_s, out_s, x_s, x_r, q_s, q_r, z_s, z_r, y_s, y_r, sl_s, sl_r, sr_s, sr_r,
-        w1_s, w1_r, w2_s, w2_r, w3_s, w3_r, t_s, t_r, a_s, a_r, u_s, u_r, o_s, o_r, v_s,
+        in_s, p_s, p_r, x_s, x_r, q_s, q_r, z_s, z_r, y_s, y_r, sl_s, sl_r, sr_s, sr_r,
+        w1_s, w1_r, w2_s, w2_r, w3_s, w3_r, t_s, t_r, a_s, a_r, u_s, u_r, v_s, v_r, o_s, o_r, b_s,
     ) = rest[len(kinds) * len(GROUPS) :]
     r, c, d = lax.axis_index("trow"), lax.axis_index("tcol"), lax.axis_index("dp")
     x, zl = lax.div(c, jnp.int32(2)), rem(c, 2)
@@ -95,10 +91,16 @@
 
     behind = rem(r - c + N, N)
 
-    @pl.when(jnp.logical_and(behind >= 1, behind <= ND - 2))
+    turned = jnp.logical_and(behind >= 1, behind <= ND - 2)
+    own_relay = jnp.logical_and(turned, c == d)
+
+    @pl.when(turned)
     def _():
         def to_source(i, _):
-            here(c, d, i)
+            @pl.when(jnp.logical_or(c != d, i != d))
+            def _():
+                here(r, d, i)
+
             return 0
 
         lax.fori_loop(0, N, to_source, 0)
@@ -130,33 +132,33 @@
 
     lane = lax.broadcasted_iota(jnp.int32, (W, W), 1)
     loads[0].wait()
-    fl[:W, :DIN] = f_ref[...].astype(F32).T.astype(BF16)
+    fl[:W, :] = f_ref[...].astype(F32).T.astype(BF16)
     loads[1].wait()
-    ph = jnp.broadcast_to(p_ref[...], (W, W)).T
-    hi = ph.astype(BF16)
-    left_over = ph - hi.astype(F32)
-    mid = left_over.astype(BF16)
-    low = (left_over - mid.astype(F32)).astype(BF16)
-    packed = jnp.where(lane == 0, hi.astype(F32), 0.0)
-    packed = jnp.where(lane == 1, mid.astype(F32), packed)
-    packed = jnp.where(lane == 2, low.astype(F32), packed)
-    fl[:W, DIN:] = packed.astype(BF16)
+    pl.semaphore_wait(barrier, 3 * (N - 1) + 1 + ND - 2 + jnp.where(r != c, 1, 0) - jnp.where(own_relay, 1, 0))
+
+    xp, xm, xo = (rem(x + i, 4) * 2 + zl for i in (1, 3, 2))
+    slots = [c, xm, xp, xo, c + other, xm + other, xp + other, xo + other]
+    ydev = (rem(r + 7, N), c, d)
+    own = fl.at[half(0)]
+
+    def quarter(buffer, slot, i):
+        return buffer.at[pl.ds(pl.multiple_of(slot * W + k * HALF + i * 32, 32), 32)]
+
+    send(own, fl.at[half(1)], x_s.at[0], x_r.at[0], (r, xp, d))
+    send(own, fl.at[half(2)], x_s.at[1], x_r.at[1], (r, xm, d))
+    for i in range(2):
+        send(quarter(fl, 0, i), quarter(fr, 0, i), y_s.at[i], y_r.at[i], ydev)
+    send(own, fl.at[half(4)], z_s.at[0], z_r.at[0], zdev)
+
+    for i in range(1, N):
+        send(p_ref, pall.at[c], p_s.at[i], p_r.at[i], (r, rem(c + i, N), d))
+    for i in range(1, ND):
+        send(p_ref, pall.at[N + i - 1], p_s.at[N + i - 1], p_r.at[N + i - 1], (rem(r + N - i, N), c, d))
+
     loads[2].wait()
     wpad[...] = jnp.zeros_like(wpad)
     wpad[:, :CLS] = w_ref[...]
     wown[...] = wpad[...].T.astype(BF16)
-
-    pl.semaphore_wait(barrier, 3 * (N - 1) + 1 + ND - 2 + jnp.where(r != c, 1, 0))
-
-    xp, xm, xo = (rem(x + i, 4) * 2 + zl for i in (1, 3, 2))
-    slots = [c, xm, xp, xo, c + other, xm + other, xp + other, xo + other]
-    ydev = (rem(r + 7, N), c, d)
-    own = fl.at[half(0)]
-    send(own, fl.at[half(1)], x_s.at[0], x_r.at[0], (r, xp, d))
-    send(own, fl.at[half(2)], x_s.at[1], x_r.at[1], (r, xm, d))
-    send(own, fr.at[half(0)], y_s.at[0], y_r.at[0], ydev)
-    send(own, fl.at[half(4)], z_s.at[0], z_r.at[0], zdev)
-
     wcols = rows(place(d), W)
     wmine = wall.at[:, wcols]
 
@@ -168,25 +170,27 @@
     def _():
         wall[:, wcols] = wown[...]
 
-    def cosines(src, n):
-        phase = src[:, DIN:].astype(F32)
-        phase = phase[:, 0:1] + phase[:, 1:2] + phase[:, 2:3]
-        angle = dot(src[:, :DIN], e_ref[...], NT) + phase
-        t = angle * INV_PERIOD
-        t = t - jnp.round(t)
-        u = t * t
-        v = jnp.full_like(u, COS[-1])
-        for q in COS[-2::-1]:
-            v = v * u + q
-        return v.astype(BF16)
+    def cosines(src, phases):
+        t = dot(src[...], e_ref[...], NT) * INV_PERIOD + jnp.concatenate(phases, axis=0)
+        v = 0.25 - jnp.abs(t - jnp.round(t))
+        u = v * v
+        w = jnp.full_like(u, SIN[-1])
+        for q in SIN[-2::-1]:
+            w = w * u + q
+        return (w * v).astype(BF16)
+
+    def phases(first, n):
+        return [pcol[:, i : i + 1] for i in range(first, first + n)]
 
     def left(first, n):
-        v = cosines(fl.at[first * W : (first + n) * W], n)
+        v = cosines(fl.at[first * W : (first + n) * W], phases(first, n) if first else [own_phase])
         for i in range(n):
             feat[rows(place(slots[first + i]), W), :] = v[i * W : (i + 1) * W]
 
     def right(first, n):
-        featr[(first + 1) * W : (first + 1 + n) * W, :] = cosines(fr.at[first * W : (first + n) * W], n)
+        featr[(first + 1) * W : (first + 1 + n) * W, :] = cosines(
+            fr.at[first * W : (first + n) * W], phases(N + first, n)
+        )
 
     def to_sib(i):
         send(fl.at[half(i)], fl.at[half(i)], sl_s.at[i], sl_r.at[i], sib)
@@ -203,26 +207,28 @@
             arrived(fl.at[half(i, 1 - k)], sl_s.at[i], sl_r.at[i])
 
     def hop_y(i):
+        for n in range(2):
+            piece = quarter(fr, i, n)
+            arrived(piece, y_s.at[2 * i + n], y_r.at[2 * i + n])
+            if i < ND - 2:
+                m = 2 * i + 2 + n
+                send(piece, quarter(fr, i + 1, n), y_s.at[m], y_r.at[m], ydev)
         piece = fr.at[half(i)]
-        arrived(piece, y_s.at[i], y_r.at[i])
-        if i < ND - 2:
-            send(piece, fr.at[half(i + 1)], y_s.at[i + 1], y_r.at[i + 1], ydev)
         send(piece, piece, sr_s.at[i], sr_r.at[i], sib)
 
     def sib_y(*which):
         for i in which:
             arrived(fr.at[half(i, 1 - k)], sr_s.at[i], sr_r.at[i])
 
+    own_phase = (jnp.broadcast_to(p_ref[...], (W, W)) * INV_PERIOD).T[:, 0:1]
     loads[4].wait()
     left(0, 1)
+    prow[...] = jnp.zeros_like(prow)
     featr[0:W, :] = feat[rows(place(c), W), :]
-
-    def quarter(slot, i):
-        return fl.at[pl.ds(pl.multiple_of(slot * W + k * HALF + i * 32, 32), 32)]
 
     for i, (slot, on) in enumerate(((1, xp), (2, xm))):
         arrived(fl.at[half(slot)], x_s.at[i], x_r.at[i])
-        send(quarter(slot, i), quarter(3, i), q_s.at[i], q_r.at[i], (r, on, d))
+        send(quarter(fl, slot, i), quarter(fl, 3, i), q_s.at[i], q_r.at[i], (r, on, d))
         to_z(slot)
         to_sib(slot)
     hop_y(0)
@@ -236,11 +242,19 @@
     for i in range(1, 4):
         send(wmine, wmine, w2_s.at[i], w2_r.at[i], (r, c, 2 * rem(h + i, 4) + k))
 
+    for i in range(1, N):
+        arrived(pall.at[rem(c + N - i, N)], p_s.at[i], p_r.at[i])
+    for i in range(N, N + ND - 1):
+        arrived(pall.at[i], p_s.at[i], p_r.at[i])
+        prow[i : i + 1, :] = pall[i]
+    for i in range(1, N):
+        prow[i : i + 1, :] = pall[slots[i]]
+    pcol[...] = (prow[...] * INV_PERIOD).T
     from_sib(1, 2)
     left(1, 2)
     hop_y(1)
     for i in range(2):
-        arrived(quarter(3, i), q_s.at[i], q_r.at[i])
+        arrived(quarter(fl, 3, i), q_s.at[i], q_r.at[i])
     to_z(3)
     to_sib(3)
     from_z(1)
@@ -262,7 +276,6 @@
     for i in range(1, N):
         to = rem(r + i, N)
         send(ts.at[rows(to, 16)], tb.at[i], t_s.at[i], t_r.at[i], (to, c, d))
-    hop_y(3)
 
     scale = 1.0 / TOTAL
 
@@ -323,11 +336,25 @@
 
             if 0 < i < ND - 1:
                 xt[i - 1] = block.T.astype(BF16)
-                send(xt.at[i - 1], gb.at[d], v_s.at[i - 1], o_r.at[d], (to, r, c))
+                send(xt.at[i - 1], xr.at[i - 1], v_s.at[i - 1], v_r.at[i - 1], (to, c, d))
+
+    def relay(i):
+        arrived(xr.at[i - 1], v_s.at[i - 1], v_r.at[i - 1])
+        to = rem(r + N - i, N)
+        stays = jnp.logical_and(to == c, d == c)
+
+        @pl.when(jnp.logical_not(stays))
+        def _():
+            copy(xr.at[i - 1], gb.at[d], b_s.at[i - 1], o_r.at[d], (r, to, c)).start()
+
+        @pl.when(stays)
+        def _():
+            gb[d] = xr[i - 1]
 
     sib_y(0, 1)
     right(0, 2)
     gram_partial(groups[0], 0, 3)
+    hop_y(3)
     step_one(groups[0])
 
     total = ts[rows(r, 16), :].astype(F32)
@@ -365,19 +392,11 @@
     step_one(g)
     hand_out(groups[1], 3, 2)
     step_two(g)
+    relay(1)
+    relay(2)
 
     delta = rem(c - r + N, N)
     eye = lax.broadcasted_iota(jnp.int32, (W, W), 0) == lane
-
-    def gram_block(i, _):
-        @pl.when(jnp.logical_or(delta >= ND, i != c))
-        def _():
-            arrived(gb.at[i], o_s.at[0], o_r.at[i])
-
-        ridge = jnp.where(jnp.logical_and(eye, jnp.logical_and(r == c, d == i)), RIDGE, 0.0)
-        gram_ref[i] = gb[i].astype(F32) + ridge
-        pltpu.make_async_copy(gram_ref.at[i], gram_hbm.at[:, rows(i, W)], out_s.at[i]).start()
-        return 0
 
     total = step_three(g)
     first = total.astype(BF16).astype(F32)
@@ -392,7 +411,15 @@
     def _():
         ub[...] = us[...]
 
-    lax.fori_loop(0, N, gram_block, 0)
+    relay(3)
+    for i in range(N):
+
+        @pl.when(jnp.where(delta < ND, i != c, jnp.logical_or(c != d, i != d)))
+        def _():
+            arrived(gb.at[i], o_s.at[0], o_r.at[i])
+
+        ridge = jnp.where(jnp.logical_and(eye, jnp.logical_and(r == c, d == i)), RIDGE, 0.0)
+        gram_ref[:, i * W : (i + 1) * W] = gb[i].astype(F32) + ridge
 
     @pl.when(r != c)
     def _():
@@ -403,8 +430,6 @@
     diag = grad[:, CLS : CLS + 1] + grad[:, CLS + 1 : CLS + 2] + RIDGE
     new = old - STEP_RATE * (grad + RIDGE * old) / diag
     new_ref[...] = new[:, :CLS]
-    last = pltpu.make_async_copy(new_ref, new_hbm, out_s.at[N])
-    last.start()
 
     for m in sends:
         m.wait_send()
@@ -420,26 +445,27 @@
         def _():
             copy(xb.at[i], xb.at[i], o_s.at[i], o_r.at[0], sib).wait_send()
 
-    def written(i, _):
-        pltpu.make_async_copy(gram_ref.at[i], gram_hbm.at[:, rows(i, W)], out_s.at[i]).wait()
-        return 0
-
-    lax.fori_loop(0, N, written, 0)
-    last.wait()
+    for i in range(1, ND - 1):
+
+        @pl.when(jnp.logical_not(jnp.logical_and(rem(r + N - i, N) == c, d == c)))
+        def _():
+            copy(xr.at[0], xr.at[0], b_s.at[i - 1], o_r.at[0], sib).wait_send()
 
 
 def shards(embeds, frequencies, phases, labels, weights):
     hbm = pl.BlockSpec(memory_space=pl.ANY)
+    vmem = pl.BlockSpec(memory_space=pltpu.VMEM)
     buffers = [
         ((ROWS, DIN), BF16),
         ((DIN, W), BF16),
         ((1, W), F32),
         ((1, ROWS), jnp.int32),
         ((W, CLS), F32),
-        ((N, W, W), F32),
-        ((W, CLS), F32),
-        ((N * W, WIDE), BF16),
-        (((ND - 1) * W, WIDE), BF16),
+        ((N + ND - 1, 1, W), F32),
+        ((W, W), F32),
+        ((W, W), F32),
+        ((N * W, DIN), BF16),
+        (((ND - 1) * W, DIN), BF16),
         ((N * W, ROWS), BF16),
         ((ND * W, ROWS), BF16),
         ((W, W), F32),
@@ -451,6 +477,7 @@
         ((N * W, W), F32),
         ((ND, W, W), BF16),
         ((ND - 2, W, W), BF16),
+        ((ND - 2, W, W), BF16),
         ((N, W, W), BF16),
         ((W, W), BF16),
         ((W, W), BF16),
@@ -460,8 +487,8 @@
     for _ in range(4):
         buffers += [((2, HALF, n), BF16) for n in GROUPS]
     sem = lambda n: pltpu.SemaphoreType.DMA((n,))
-    sems = [sem(7)] * (2 * len(GROUPS)) + [sem(5), sem(N + 1)]
-    for n in (2, 2, 4, 4, N, 4, 1, 4, 4, N, N, 1):
+    sems = [sem(7)] * (2 * len(GROUPS)) + [sem(5), sem(N + ND - 1), sem(N + ND - 1)]
+    for n in (2, 2, 4, 2 * ND - 2, N, 4, 1, 4, 4, N, N, 1, ND - 2):
         sems += [sem(n), sem(n)]
     sems += [sem(ND), sem(N), sem(ND - 2)]
     return pl.pallas_call(
@@ -471,7 +498,7 @@
             jax.ShapeDtypeStruct((W, CLS), F32),
         ),
         in_specs=[hbm] * 5,
-        out_specs=(hbm, hbm),
+        out_specs=(vmem, vmem),
         scratch_shapes=[pltpu.VMEM(*b) for b in buffers] + sems,
         compiler_params=pltpu.CompilerParams(
             collective_id=0, has_side_effects=True, vmem_limit_bytes=56 * 2**20

time: 79 us -> 75.6 us (0.957)
  the two profiles are of different devices: /device:TPU:22 before, /device:TPU:14 now
where the time goes in v3:
time: 75.6 us; the launch traced here: 75.4 us
  Pallas kernels  71.4 us (94%)
  local copies, waits for them, and re-layouts  3.36 us (4%)
    pallas_call x1, Pallas kernels, shards(): pl.pallas_call(kernel, out_shape=(jax.ShapeDtypeStruct((W, N * W), F32),...  71.4 us
    unnamed x2, local copies, waits for them, and re-layouts  3.36 us

profile of v3, /device:TPU:14, one launch (start us, length us, event | category | flops | bytes accessed | tf_op | source)
XLA Modules:
  0.0 75.4 jit_solution(11147832169299672977)
XLA Ops:
  0.6 71.4 %shard_map.68 = (f32[128,1024]{1,0:T(8,128)}, f32[128,125]{1,0:T(8,128)}) custom-call(bf16[1024,1024]{1,0:T(8,128)(2,1)} %e_hbm.1, bf16[1024,128]{1,0:T(8,128)(2,1)} %f_hbm.1, f32[1,128]{1,0:T(1,128)} %bitcast.3, s32[1,1024]{1,0:T(1,128)} %bitcast.2, f32[128,125]{1,0:T(8,128)} %w_hbm.1), custom_call_target="tpu_custom_call" | custom-call | tf_op jit(solution)/shard_map/pallas_call | solution.py:494
  72.0 1.9 %copy.9 = f32[128,1024]{1,0:T(8,128)} copy(f32[128,1024]{1,0:T(8,128)} %get-tuple-element.4) | data formatting | bytes 1048576
  73.9 1.5 %copy.10 = f32[128,125]{1,0:T(8,128)} copy(f32[128,125]{1,0:T(8,128)} %get-tuple-element.5) | data formatting | bytes 128000

commit v4 on v3

--- a/solution.py
+++ b/solution.py
@@ -53,7 +53,7 @@
 def kernel(
     e_hbm, f_hbm, p_hbm, l_hbm, w_hbm, gram_ref, new_ref,
     e_ref, f_ref, p_ref, l_ref, w_ref, pall, prow, pcol,
-    fl, fr, feat, featr, wpad, wown, wall, ts, tb, st, ulab, xb, xt, xr, gb, us, ub, *rest
+    fl, fr, feat, featr, wpad, wown, wall, ts, tb, st, ulab, xb, xt, xr, gb, us, ub, uq, *rest
 ):
     kinds = ("gs", "gr", "gsum", "gb16", "ra", "rb", "cs", "rc", "sem_s", "sem_r")
     groups = [dict(zip(kinds, rest[i :: len(GROUPS)])) for i in range(len(GROUPS))]
@@ -111,7 +111,7 @@
             ((f_hbm, f_ref), (p_hbm, p_ref), (w_hbm, w_ref), (l_hbm, l_ref), (e_hbm, e_ref))
         )
     ]
-    for m in loads:
+    for m in loads[:3]:
         m.start()
 
     def copy(src, dst, s, t, dev):
@@ -132,6 +132,8 @@
 
     lane = lax.broadcasted_iota(jnp.int32, (W, W), 1)
     loads[0].wait()
+    for m in loads[3:]:
+        m.start()
     fl[:W, :] = f_ref[...].astype(F32).T.astype(BF16)
     loads[1].wait()
     pl.semaphore_wait(barrier, 3 * (N - 1) + 1 + ND - 2 + jnp.where(r != c, 1, 0) - jnp.where(own_relay, 1, 0))
@@ -146,8 +148,7 @@
 
     send(own, fl.at[half(1)], x_s.at[0], x_r.at[0], (r, xp, d))
     send(own, fl.at[half(2)], x_s.at[1], x_r.at[1], (r, xm, d))
-    for i in range(2):
-        send(quarter(fl, 0, i), quarter(fr, 0, i), y_s.at[i], y_r.at[i], ydev)
+    send(own, fr.at[half(0)], y_s.at[0], y_r.at[0], ydev)
     send(own, fl.at[half(4)], z_s.at[0], z_r.at[0], zdev)
 
     for i in range(1, N):
@@ -207,13 +208,10 @@
             arrived(fl.at[half(i, 1 - k)], sl_s.at[i], sl_r.at[i])
 
     def hop_y(i):
-        for n in range(2):
-            piece = quarter(fr, i, n)
-            arrived(piece, y_s.at[2 * i + n], y_r.at[2 * i + n])
-            if i < ND - 2:
-                m = 2 * i + 2 + n
-                send(piece, quarter(fr, i + 1, n), y_s.at[m], y_r.at[m], ydev)
         piece = fr.at[half(i)]
+        arrived(piece, y_s.at[i], y_r.at[i])
+        if i < ND - 2:
+            send(piece, fr.at[half(i + 1)], y_s.at[i + 1], y_r.at[i + 1], ydev)
         send(piece, piece, sr_s.at[i], sr_r.at[i], sib)
 
     def sib_y(*which):
@@ -233,14 +231,6 @@
         to_sib(slot)
     hop_y(0)
     from_z(0)
-
-    @pl.when(r != c)
-    def _():
-        arrived(wmine, w1_s.at[0], w1_r.at[0])
-
-    send(wmine, wmine, w3_s.at[0], w3_r.at[0], sib)
-    for i in range(1, 4):
-        send(wmine, wmine, w2_s.at[i], w2_r.at[i], (r, c, 2 * rem(h + i, 4) + k))
 
     for i in range(1, N):
         arrived(pall.at[rem(c + N - i, N)], p_s.at[i], p_r.at[i])
@@ -257,18 +247,28 @@
         arrived(quarter(fl, 3, i), q_s.at[i], q_r.at[i])
     to_z(3)
     to_sib(3)
+    @pl.when(r != c)
+    def _():
+        arrived(wmine, w1_s.at[0], w1_r.at[0])
+
+    send(wmine, wmine, w3_s.at[0], w3_r.at[0], sib)
+    for i in range(1, 4):
+        send(wmine, wmine, w2_s.at[i], w2_r.at[i], (r, c, 2 * rem(h + i, 4) + k))
+
     from_z(1)
     from_z(2)
+    from_sib(3, 4)
+    left(3, 2)
+    from_sib(5, 6)
+    left(5, 2)
     for i in range(1, 4):
         piece = wall.at[:, rows(place(2 * rem(h + 4 - i, 4) + k), W)]
         arrived(piece, w2_s.at[i], w2_r.at[i])
         send(piece, piece, w3_s.at[i], w3_r.at[i], sib)
-    from_sib(3, 4)
-    left(3, 2)
+    from_z(3)
     hop_y(2)
-    from_z(3)
-    from_sib(5, 6, 7)
-    left(5, 3)
+    from_sib(7)
+    left(7, 1)
 
     for i in range(4):
         arrived(wall.at[:, rows(place(2 * rem(h + 4 - i, 4) + 1 - k), W)], w3_s.at[i], w3_r.at[i])
@@ -354,9 +354,12 @@
     sib_y(0, 1)
     right(0, 2)
     gram_partial(groups[0], 0, 3)
+    step_one(groups[0])
     hop_y(3)
-    step_one(groups[0])
-
+
+    sib_y(2, 3)
+    right(2, 2)
+    step_two(groups[0])
     total = ts[rows(r, 16), :].astype(F32)
     for i in range(1, N):
         arrived(tb.at[i], t_s.at[i], t_r.at[i])
@@ -366,9 +369,6 @@
     for i in range(1, N):
         send(strip, strip, a_s.at[i], a_r.at[i], (rem(r + i, N), c, d))
 
-    sib_y(2, 3)
-    right(2, 2)
-    step_two(groups[0])
     gram_partial(groups[1], 3, 2)
     step_one(groups[1])
 
@@ -379,8 +379,8 @@
     diag = jnp.sum(own_f * own_f, axis=1, keepdims=True)
     lane_u = lax.broadcasted_iota(jnp.int32, (N * W, W), 1)
     ulab[...] = jnp.where(lane_u == CLS, diag, -C * dot(feat[...], onehot, NT)) * scale
+    step_two(groups[1])
     hand_out(groups[0], 0, 3)
-    step_two(groups[1])
 
     for i in range(1, N):
         arrived(st.at[rows(rem(r + N - i, N), 16)], a_s.at[i], a_r.at[i])
@@ -389,16 +389,23 @@
     g["gs"][...] = ulab[rows(1 - k, 512), :].astype(BF16)
     swap(g)
     g["gsum"][...] = ulab[rows(k, 512), :]
-    step_one(g)
+    arrived(g["gr"], g["sem_s"].at[0], g["sem_r"].at[0])
+    g["gsum"][...] = g["gsum"][...] + g["gr"][...].astype(F32)
+    g["gb16"][...] = g["gsum"][...].astype(BF16)
+    for i in range(1, 4):
+        to = rem(h + i, 4)
+        send(g["gb16"].at[rows(to, W)], uq.at[i - 1], g["sem_s"].at[i], g["sem_r"].at[i], (r, c, 2 * to + k))
     hand_out(groups[1], 3, 2)
-    step_two(g)
     relay(1)
     relay(2)
 
     delta = rem(c - r + N, N)
     eye = lax.broadcasted_iota(jnp.int32, (W, W), 0) == lane
 
-    total = step_three(g)
+    total = g["gsum"][rows(h, W), :]
+    for i in range(1, 4):
+        arrived(uq.at[i - 1], g["sem_s"].at[i], g["sem_r"].at[i])
+        total = total + uq[i - 1].astype(F32)
     first = total.astype(BF16).astype(F32)
     second = (total - first)[:, CLS : CLS + 1]
     us[...] = jnp.where(lane == CLS + 1, second, total).astype(BF16)
@@ -481,6 +488,7 @@
         ((N, W, W), BF16),
         ((W, W), BF16),
         ((W, W), BF16),
+        ((3, W, W), BF16),
     ]
     for dtype in (BF16, BF16, F32, BF16):
         buffers += [((4 * W, n), dtype) for n in GROUPS]
@@ -488,7 +496,7 @@
         buffers += [((2, HALF, n), BF16) for n in GROUPS]
     sem = lambda n: pltpu.SemaphoreType.DMA((n,))
     sems = [sem(7)] * (2 * len(GROUPS)) + [sem(5), sem(N + ND - 1), sem(N + ND - 1)]
-    for n in (2, 2, 4, 2 * ND - 2, N, 4, 1, 4, 4, N, N, 1, ND - 2):
+    for n in (2, 2, 4, ND - 1, N, 4, 1, 4, 4, N, N, 1, ND - 2):
         sems += [sem(n), sem(n)]
     sems += [sem(ND), sem(N), sem(ND - 2)]
     return pl.pallas_call(

time: 75.6 us -> 74.4 us (0.984)
  Pallas kernels: 71.4 us -> 70.2 us
    pallas_call x1, Pallas kernels: 71.4 us -> 70.2 us  [shards(): pl.pallas_call(kernel, out_shape=(jax.ShapeDtypeStruct((W, N * W), F32),...]
where the time goes in v4:
time: 74.4 us; the launch traced here: 74.2 us
  Pallas kernels  70.2 us (94%)
  local copies, waits for them, and re-layouts  3.36 us (5%)
    pallas_call x1, Pallas kernels, shards(): pl.pallas_call(kernel, out_shape=(jax.ShapeDtypeStruct((W, N * W), F32),...  70.2 us
    unnamed x2, local copies, waits for them, and re-layouts  3.36 us

profile of v4, /device:TPU:14, one launch (start us, length us, event | category | flops | bytes accessed | tf_op | source)
XLA Modules:
  0.0 74.2 jit_solution(17736763407313767522)
XLA Ops:
  0.6 70.2 %shard_map.68 = (f32[128,1024]{1,0:T(8,128)}, f32[128,125]{1,0:T(8,128)}) custom-call(bf16[1024,1024]{1,0:T(8,128)(2,1)} %e_hbm.1, bf16[1024,128]{1,0:T(8,128)(2,1)} %f_hbm.1, f32[1,128]{1,0:T(1,128)} %bitcast.3, s32[1,1024]{1,0:T(1,128)} %bitcast.2, f32[128,125]{1,0:T(8,128)} %w_hbm.1), custom_call_target="tpu_custom_call" | custom-call | tf_op jit(solution)/shard_map/pallas_call | solution.py:502
  70.8 1.9 %copy.9 = f32[128,1024]{1,0:T(8,128)} copy(f32[128,1024]{1,0:T(8,128)} %get-tuple-element.4) | data formatting | bytes 1048576
  72.7 1.5 %copy.10 = f32[128,125]{1,0:T(8,128)} copy(f32[128,125]{1,0:T(8,128)} %get-tuple-element.5) | data formatting | bytes 128000

commit v5 on v4

--- a/solution.py
+++ b/solution.py
@@ -146,9 +146,9 @@
     def quarter(buffer, slot, i):
         return buffer.at[pl.ds(pl.multiple_of(slot * W + k * HALF + i * 32, 32), 32)]
 
+    send(own, fr.at[half(0)], y_s.at[0], y_r.at[0], ydev)
     send(own, fl.at[half(1)], x_s.at[0], x_r.at[0], (r, xp, d))
     send(own, fl.at[half(2)], x_s.at[1], x_r.at[1], (r, xm, d))
-    send(own, fr.at[half(0)], y_s.at[0], y_r.at[0], ydev)
     send(own, fl.at[half(4)], z_s.at[0], z_r.at[0], zdev)
 
     for i in range(1, N):
@@ -224,12 +224,12 @@
     prow[...] = jnp.zeros_like(prow)
     featr[0:W, :] = feat[rows(place(c), W), :]
 
+    hop_y(0)
     for i, (slot, on) in enumerate(((1, xp), (2, xm))):
         arrived(fl.at[half(slot)], x_s.at[i], x_r.at[i])
         send(quarter(fl, slot, i), quarter(fl, 3, i), q_s.at[i], q_r.at[i], (r, on, d))
         to_z(slot)
         to_sib(slot)
-    hop_y(0)
     from_z(0)
 
     for i in range(1, N):

time: 74.4 us -> 74.2 us (level)
  the two profiles are of different devices: /device:TPU:14 before, /device:TPU:1 now
where the time goes in v5:
time: 74.2 us; the launch traced here: 74 us
  Pallas kernels  70 us (94%)
  local copies, waits for them, and re-layouts  3.36 us (5%)
    pallas_call x1, Pallas kernels, shards(): pl.pallas_call(kernel, out_shape=(jax.ShapeDtypeStruct((W, N * W), F32),...  70 us
    unnamed x2, local copies, waits for them, and re-layouts  3.36 us

profile of v5, /device:TPU:1, one launch (start us, length us, event | category | flops | bytes accessed | tf_op | source)
XLA Modules:
  0.0 74.0 jit_solution(14883214370348621451)
XLA Ops:
  0.6 70.0 %shard_map.68 = (f32[128,1024]{1,0:T(8,128)}, f32[128,125]{1,0:T(8,128)}) custom-call(bf16[1024,1024]{1,0:T(8,128)(2,1)} %e_hbm.1, bf16[1024,128]{1,0:T(8,128)(2,1)} %f_hbm.1, f32[1,128]{1,0:T(1,128)} %bitcast.3, s32[1,1024]{1,0:T(1,128)} %bitcast.2, f32[128,125]{1,0:T(8,128)} %w_hbm.1), custom_call_target="tpu_custom_call" | custom-call | tf_op jit(solution)/shard_map/pallas_call | solution.py:502
  70.6 1.9 %copy.9 = f32[128,1024]{1,0:T(8,128)} copy(f32[128,1024]{1,0:T(8,128)} %get-tuple-element.4) | data formatting | bytes 1048576
  72.5 1.5 %copy.10 = f32[128,125]{1,0:T(8,128)} copy(f32[128,125]{1,0:T(8,128)} %get-tuple-element.5) | data formatting | bytes 128000
